TPU v7x, 512 devices: a whole 4x8x8 slice. The times are simulated.
512 devices in a mesh: tm: 32 (over x, y), cp: 16 (over z, core).
Axes of the slice: x: 4, y: 8, z: 8, core: 2. Of those that a mesh axis runs over, the one named last changes fastest.
Arguments:
- echoes: bfloat16 [2, 128, 524288], P(None, 'cp', 'tm'), may hold values from -6 to 6
Outputs:
- channels: bfloat16 [2, 128, 64, 8192], P(None, 'cp', 'tm')
All inputs are finite; a program needn't handle non-finite values.
Results may differ from a plain program's by a relative error of at most 0.0068.
Values may be sent and summed in bfloat16 or wider, within the bound.
A program may use at most 64 MiB of HBM per device.

v0:
```python
import math

import jax
import jax.numpy as jnp
import ml_dtypes
import numpy as np
from jax import lax
from jax.experimental import pallas as pl
from jax.experimental.pallas import tpu as pltpu
from jax.sharding import PartitionSpec as P

CHIRP = 1024
BANDS = 64
TAPS = 4096
MESH = pl.DeviceIdType.MESH

FRAME = 128
SPAN = 41
HALO = SPAN - 1
WEIGHT_PARTS = 4


def rounded(values):
    return np.asarray(values, np.float64).astype(ml_dtypes.bfloat16).astype(np.float64)


def weights():
    lag = np.arange(CHIRP)
    phase = math.pi * ((lag - CHIRP // 2) ** 2 % (2 * CHIRP)) / CHIRP
    scale = 1.0 / math.sqrt(CHIRP)
    chirp = rounded(np.cos(phase) * scale) + 1j * rounded(np.sin(phase) * scale)
    tap = np.arange(TAPS)
    window = 0.5 - 0.5 * np.cos(2.0 * np.pi * (tap + 0.5) / TAPS)
    prototype = rounded(np.sinc((tap - (TAPS - 1) / 2.0) / BANDS) * window / math.sqrt(BANDS))
    column = np.arange(BANDS)
    angle = 2.0 * np.pi * (column[:, None] * column[None, :] % BANDS) / BANDS
    table = rounded(np.cos(angle)) - 1j * rounded(np.sin(angle))
    modulated = prototype[None, :] * np.tile(table, (1, TAPS // BANDS))
    length = 2 * TAPS
    filters = np.fft.ifft(
        np.fft.fft(modulated, length, axis=1) * np.fft.fft(chirp[::-1], length)[None, :], axis=1
    )[:, : TAPS + CHIRP - 1]
    samples = SPAN * FRAME
    placed = np.zeros((2, samples, BANDS), np.complex128)
    for parity in range(2):
        first = (SPAN - 1) * FRAME + (parity + 1) * BANDS - (TAPS + CHIRP - 1)
        placed[parity, first : first + TAPS + CHIRP - 1] = filters.T
    real, imag = placed.real, placed.imag
    parts = np.stack(
        [np.stack([real, imag], axis=2), np.stack([-imag, real], axis=2)]
    )
    parts = parts.reshape(2, 2, SPAN, FRAME, 2, BANDS // 2, 2)
    parts = parts.transpose(2, 0, 3, 1, 6, 4, 5)
    return parts.reshape(SPAN, 2 * FRAME, 4 * BANDS).astype(np.float32).astype(ml_dtypes.bfloat16)


def kernel(
    count, x_ref, w_ref, o_ref, own, halo, weight, pairs, total, times, turned, outgoing,
    own_sem, weight_sem, halo_send, halo_recv, send_sem, recv_sem, local_sem,
):
    me = lax.axis_index("tm")
    frames = own.shape[1] // FRAME
    half = frames // 2
    quarter = half // 2
    steps = 2 * frames

    load = pltpu.make_async_copy(x_ref, own, own_sem)
    load.start()
    loads = []
    bounds = [SPAN * i // WEIGHT_PARTS for i in range(WEIGHT_PARTS + 1)]
    for i in range(WEIGHT_PARTS):
        piece = pl.ds(bounds[i], bounds[i + 1] - bounds[i])
        loads.append(
            pltpu.make_async_copy(w_ref.at[piece], weight.at[piece], weight_sem.at[i])
        )
        loads[-1].start()

    barrier = pltpu.get_barrier_semaphore()
    for shift in range(1, count):
        pl.semaphore_signal(
            barrier, inc=1, device_id={"tm": lax.rem(me + shift, count)}, device_id_type=MESH
        )
    pl.semaphore_wait(barrier, count - 1)

    edge = pltpu.make_async_remote_copy(
        src_ref=x_ref.at[:, pl.ds((frames - HALO) * FRAME, HALO * FRAME)],
        dst_ref=halo,
        send_sem=halo_send,
        recv_sem=halo_recv,
        device_id={"tm": lax.rem(me + 1, count)},
        device_id_type=MESH,
    )

    @pl.when(me < count - 1)
    def _():
        edge.start()

    def pair(earlier, later):
        earlier, later = earlier.astype(jnp.float32), later.astype(jnp.float32)
        return jnp.concatenate(
            [
                jnp.concatenate([earlier[:8], later[:8]], axis=0),
                jnp.concatenate([earlier[8:], later[8:]], axis=0),
            ],
            axis=1,
        ).astype(jnp.bfloat16)

    def frame_of(ref, index):
        return ref[:, pl.ds(pl.multiple_of(index * FRAME, FRAME), FRAME)]

    def pair_own(first, last):
        def one(index, carry):
            pairs[HALO + index] = pair(frame_of(own, index), frame_of(own, index + quarter))
            return carry

        lax.fori_loop(first, last, one, 0, unroll=8)

    def pair_halo():
        def both(index, carry):
            pairs[index] = pair(frame_of(halo, index), frame_of(halo, index + quarter))
            return carry

        def mixed(index, carry):
            pairs[index] = pair(frame_of(halo, index), frame_of(own, index + quarter - HALO))
            return carry

        lax.fori_loop(0, HALO - quarter, both, 0, unroll=8)
        lax.fori_loop(HALO - quarter, HALO, mixed, 0, unroll=8)

    load.wait()
    pair_own(half - HALO, half + quarter)

    def one_half(turn, carry):
        side = 1 - turn
        @pl.when(turn == 1)
        def _():
            pair_own(0, half - HALO)

            @pl.when(me > 0)
            def _():
                edge.wait_recv()

            @pl.when(me == 0)
            def _():
                halo[...] = jnp.zeros_like(halo)

            pair_halo()

        for i in range(WEIGHT_PARTS):
            @pl.when(turn == 0)
            def _():
                loads[i].wait()

            lag = bounds[i]
            amount = bounds[i + 1] - bounds[i]
            first = side * half
            left = jnp.concatenate(
                [
                    pairs[pl.ds(first + lag + j, quarter)].reshape(quarter * 16, 2 * FRAME)
                    for j in range(amount)
                ],
                axis=1,
            )
            right = weight[pl.ds(lag, amount)].reshape(amount * 2 * FRAME, 4 * BANDS)
            product = jnp.dot(left, right, preferred_element_type=jnp.float32)
            if i == 0:
                total[...] = product
            else:
                total[...] += product

        for v in range(quarter):
            for late in range(2):
                for parity in range(2):
                    row = ((late * quarter + v) * 2 + parity) * 8
                    times[row : row + 8, :] = total[
                        v * 16 + late * 8 : v * 16 + late * 8 + 8, parity * 128 : parity * 128 + 128
                    ]
        for r in range(8):
            across = times[pl.ds(r, frames, stride=8), :].T
            for band in range(2):
                turned[pl.ds(2 * r + band, 2 * count, stride=16), :] = across[
                    band * 64 : band * 64 + 64
                ]
        outgoing[side] = turned[...].astype(jnp.bfloat16).reshape(2, count, 16, frames)

        start = pl.multiple_of(me * steps + side * frames, frames)
        for shift in range(1, count):
            to = lax.rem(me + shift, count)
            pltpu.make_async_remote_copy(
                src_ref=outgoing.at[side, :, to],
                dst_ref=o_ref.at[:, :, pl.ds(start, frames)],
                send_sem=send_sem.at[side, shift],
                recv_sem=recv_sem.at[side, shift],
                device_id={"tm": to},
                device_id_type=MESH,
            ).start()
        pltpu.make_async_copy(
            outgoing.at[side, :, me], o_ref.at[:, :, pl.ds(start, frames)], local_sem.at[side]
        ).start()
        return carry

    lax.fori_loop(0, 2, one_half, 0)

    @pl.when(me < count - 1)
    def _():
        edge.wait_send()

    for turn in range(2):
        side = 1 - turn
        start = pl.multiple_of(me * steps + side * frames, frames)
        for shift in range(1, count):
            to = lax.rem(me + shift, count)
            pltpu.make_async_remote_copy(
                src_ref=outgoing.at[side, :, to],
                dst_ref=o_ref.at[:, :, pl.ds(start, frames)],
                send_sem=send_sem.at[side, shift],
                recv_sem=recv_sem.at[side, shift],
                device_id={"tm": to},
                device_id_type=MESH,
            ).wait()
        pltpu.make_async_copy(
            outgoing.at[side, :, me], o_ref.at[:, :, pl.ds(start, frames)], local_sem.at[side]
        ).wait()


def solution(mesh):
    count = mesh.shape["tm"]
    table = weights()

    def shards(echoes):
        parts, rows, samples = echoes.shape
        frames = samples // FRAME
        quarter = frames // 4
        result = pl.pallas_call(
            lambda *refs: kernel(count, *refs),
            out_shape=jax.ShapeDtypeStruct((2, 16, count * 2 * frames), jnp.bfloat16),
            in_specs=[pl.BlockSpec(memory_space=pl.ANY)] * 2,
            out_specs=pl.BlockSpec(memory_space=pl.ANY),
            scratch_shapes=[
                pltpu.VMEM((16, samples), jnp.bfloat16),
                pltpu.VMEM((16, HALO * FRAME), jnp.bfloat16),
                pltpu.VMEM(table.shape, jnp.bfloat16),
                pltpu.VMEM((HALO + frames - quarter, 16, 2 * FRAME), jnp.bfloat16),
                pltpu.VMEM((quarter * 16, 4 * BANDS), jnp.float32),
                pltpu.VMEM((frames * 8, 2 * BANDS), jnp.float32),
                pltpu.VMEM((2 * count * 16, frames), jnp.float32),
                pltpu.VMEM((2, 2, count, 16, frames), jnp.bfloat16),
                pltpu.SemaphoreType.DMA,
                pltpu.SemaphoreType.DMA((WEIGHT_PARTS,)),
                pltpu.SemaphoreType.DMA,
                pltpu.SemaphoreType.DMA,
                pltpu.SemaphoreType.DMA((2, count)),
                pltpu.SemaphoreType.DMA((2, count)),
                pltpu.SemaphoreType.DMA((2,)),
            ],
            compiler_params=pltpu.CompilerParams(
                collective_id=0, has_side_effects=True, vmem_limit_bytes=60 << 20
            ),
            name="radar",
        )(echoes.reshape(parts * rows, samples), jnp.asarray(table))
        return result.reshape(2, rows, 2, count * 2 * frames)

    return jax.shard_map(
        shards,
        mesh=mesh,
        in_specs=(P(None, "cp", "tm"),),
        out_specs=P(None, "cp", "tm", None),
        check_vma=False,
    )
```

profile of v0, /device:TPU:2, one launch (start us, length us, event | category | flops | bytes accessed | tf_op | source)
XLA Modules:
  0.0 33.2 jit_solution(13359344216855206630)
XLA Ops:
  0.0 31.0 %radar.1 = bf16[2,16,8192]{2,1,0:T(8,128)(2,1)} custom-call(bf16[16,16384]{1,0:T(8,128)(2,1)} %bitcast.1, bf16[41,256,256]{2,1,0:T(8,128)(2,1)} %constant.2.clone.refs_1_), custom_call_target="tpu_custom_call" | custom-call | tf_op jit(solution)/shard_map/radar/pallas_call | solution.py:234
  31.0 2.2 %reshape.7 = bf16[2,8,2,8192]{3,2,1,0:T(2,128)(2,1)} reshape(bf16[2,16,8192]{2,1,0:T(8,128)(2,1)} %radar.1) | data formatting | bytes 1048576 | tf_op jit(solution)/shard_map/reshape | solution.py:261
where the time goes:
time: 33.3 us; the launch traced here: 33.2 us
  Pallas kernels  31 us (93%)
  local copies, waits for them, and re-layouts  2.17 us (7%)
    pallas_call x1, Pallas kernels, shards(): pl.pallas_call(lambda *refs: kernel(count, *refs), out_shape=jax.ShapeDty...  31 us
    reshape x1, local copies, waits for them, and re-layouts, shards(): return result.reshape(2, rows, 2, count * 2 * frames)  2.17 us

commit v1 on v0

--- a/solution.py
+++ b/solution.py
@@ -17,7 +17,8 @@
 FRAME = 128
 SPAN = 41
 HALO = SPAN - 1
-WEIGHT_PARTS = 4
+GROUP = 10
+GROUPS = (SPAN - 1) // GROUP
 
 
 def rounded(values):
@@ -66,21 +67,21 @@
 
     load = pltpu.make_async_copy(x_ref, own, own_sem)
     load.start()
-    loads = []
-    bounds = [SPAN * i // WEIGHT_PARTS for i in range(WEIGHT_PARTS + 1)]
-    for i in range(WEIGHT_PARTS):
-        piece = pl.ds(bounds[i], bounds[i + 1] - bounds[i])
-        loads.append(
-            pltpu.make_async_copy(w_ref.at[piece], weight.at[piece], weight_sem.at[i])
-        )
-        loads[-1].start()
+
+    def weight_load(group):
+        piece = pl.ds(0, 1) if group is None else pl.ds(1 + group * GROUP, GROUP)
+        sem = weight_sem.at[GROUPS if group is None else group]
+        return pltpu.make_async_copy(w_ref.at[piece], weight.at[piece], sem)
+
+    weight_load(None).start()
+    for group in range(GROUPS):
+        weight_load(group).start()
 
     barrier = pltpu.get_barrier_semaphore()
     for shift in range(1, count):
         pl.semaphore_signal(
             barrier, inc=1, device_id={"tm": lax.rem(me + shift, count)}, device_id_type=MESH
         )
-    pl.semaphore_wait(barrier, count - 1)
 
     edge = pltpu.make_async_remote_copy(
         src_ref=x_ref.at[:, pl.ds((frames - HALO) * FRAME, HALO * FRAME)],
@@ -91,9 +92,12 @@
         device_id_type=MESH,
     )
 
-    @pl.when(me < count - 1)
-    def _():
-        edge.start()
+    def greet():
+        pl.semaphore_wait(barrier, count - 1)
+
+        @pl.when(me < count - 1)
+        def _():
+            edge.start()
 
     def pair(earlier, later):
         earlier, later = earlier.astype(jnp.float32), later.astype(jnp.float32)
@@ -146,14 +150,9 @@
 
             pair_halo()
 
-        for i in range(WEIGHT_PARTS):
-            @pl.when(turn == 0)
-            def _():
-                loads[i].wait()
-
-            lag = bounds[i]
-            amount = bounds[i + 1] - bounds[i]
-            first = side * half
+        first = side * half
+
+        def product(lag, amount):
             left = jnp.concatenate(
                 [
                     pairs[pl.ds(first + lag + j, quarter)].reshape(quarter * 16, 2 * FRAME)
@@ -162,11 +161,28 @@
                 axis=1,
             )
             right = weight[pl.ds(lag, amount)].reshape(amount * 2 * FRAME, 4 * BANDS)
-            product = jnp.dot(left, right, preferred_element_type=jnp.float32)
-            if i == 0:
-                total[...] = product
-            else:
-                total[...] += product
+            return jnp.dot(left, right, preferred_element_type=jnp.float32)
+
+        @pl.when(turn == 0)
+        def _():
+            weight_load(None).wait()
+
+        total[...] = product(0, 1)
+
+        def one_group(group, carry):
+            @pl.when(turn == 0)
+            def _():
+                weight_load(group).wait()
+
+            total[...] += product(1 + group * GROUP, GROUP)
+
+            @pl.when((turn == 0) & (group == 0))
+            def _():
+                greet()
+
+            return carry
+
+        lax.fori_loop(0, GROUPS, one_group, 0)
 
         for v in range(quarter):
             for late in range(2):
@@ -181,21 +197,21 @@
                 turned[pl.ds(2 * r + band, 2 * count, stride=16), :] = across[
                     band * 64 : band * 64 + 64
                 ]
-        outgoing[side] = turned[...].astype(jnp.bfloat16).reshape(2, count, 16, frames)
+        outgoing[side] = turned[...].astype(jnp.bfloat16).reshape(2, count, 8, 2, frames)
 
         start = pl.multiple_of(me * steps + side * frames, frames)
         for shift in range(1, count):
             to = lax.rem(me + shift, count)
             pltpu.make_async_remote_copy(
                 src_ref=outgoing.at[side, :, to],
-                dst_ref=o_ref.at[:, :, pl.ds(start, frames)],
+                dst_ref=o_ref.at[:, :, :, pl.ds(start, frames)],
                 send_sem=send_sem.at[side, shift],
                 recv_sem=recv_sem.at[side, shift],
                 device_id={"tm": to},
                 device_id_type=MESH,
             ).start()
         pltpu.make_async_copy(
-            outgoing.at[side, :, me], o_ref.at[:, :, pl.ds(start, frames)], local_sem.at[side]
+            outgoing.at[side, :, me], o_ref.at[:, :, :, pl.ds(start, frames)], local_sem.at[side]
         ).start()
         return carry
 
@@ -212,14 +228,14 @@
             to = lax.rem(me + shift, count)
             pltpu.make_async_remote_copy(
                 src_ref=outgoing.at[side, :, to],
-                dst_ref=o_ref.at[:, :, pl.ds(start, frames)],
+                dst_ref=o_ref.at[:, :, :, pl.ds(start, frames)],
                 send_sem=send_sem.at[side, shift],
                 recv_sem=recv_sem.at[side, shift],
                 device_id={"tm": to},
                 device_id_type=MESH,
             ).wait()
         pltpu.make_async_copy(
-            outgoing.at[side, :, me], o_ref.at[:, :, pl.ds(start, frames)], local_sem.at[side]
+            outgoing.at[side, :, me], o_ref.at[:, :, :, pl.ds(start, frames)], local_sem.at[side]
         ).wait()
 
 
@@ -233,9 +249,9 @@
         quarter = frames // 4
         result = pl.pallas_call(
             lambda *refs: kernel(count, *refs),
-            out_shape=jax.ShapeDtypeStruct((2, 16, count * 2 * frames), jnp.bfloat16),
+            out_shape=pltpu.VMEM((2, rows, 2, count * 2 * frames), jnp.bfloat16),
             in_specs=[pl.BlockSpec(memory_space=pl.ANY)] * 2,
-            out_specs=pl.BlockSpec(memory_space=pl.ANY),
+            out_specs=pl.BlockSpec(memory_space=pltpu.VMEM),
             scratch_shapes=[
                 pltpu.VMEM((16, samples), jnp.bfloat16),
                 pltpu.VMEM((16, HALO * FRAME), jnp.bfloat16),
@@ -244,9 +260,9 @@
                 pltpu.VMEM((quarter * 16, 4 * BANDS), jnp.float32),
                 pltpu.VMEM((frames * 8, 2 * BANDS), jnp.float32),
                 pltpu.VMEM((2 * count * 16, frames), jnp.float32),
-                pltpu.VMEM((2, 2, count, 16, frames), jnp.bfloat16),
+                pltpu.VMEM((2, 2, count, 8, 2, frames), jnp.bfloat16),
                 pltpu.SemaphoreType.DMA,
-                pltpu.SemaphoreType.DMA((WEIGHT_PARTS,)),
+                pltpu.SemaphoreType.DMA((GROUPS + 1,)),
                 pltpu.SemaphoreType.DMA,
                 pltpu.SemaphoreType.DMA,
                 pltpu.SemaphoreType.DMA((2, count)),
@@ -258,7 +274,7 @@
             ),
             name="radar",
         )(echoes.reshape(parts * rows, samples), jnp.asarray(table))
-        return result.reshape(2, rows, 2, count * 2 * frames)
+        return result
 
     return jax.shard_map(
         shards,

time: 33.3 us -> 29.9 us (0.90)
  the two profiles are of different devices: /device:TPU:2 before, /device:TPU:8 now
where the time goes in v1:
time: 29.9 us; the launch traced here: 29.8 us
  Pallas kernels  29 us (97%)
  local copies, waits for them, and re-layouts  0.8 us (3%)
    pallas_call x1, Pallas kernels, shards(): pl.pallas_call(lambda *refs: kernel(count, *refs), out_shape=pltpu.VMEM((...  29 us
    unnamed x1, local copies, waits for them, and re-layouts  0.8 us

profile of v1, /device:TPU:8, one launch (start us, length us, event | category | flops | bytes accessed | tf_op | source)
XLA Modules:
  0.0 29.8 jit_solution(14353083884033596033)
XLA Ops:
  0.0 29.0 %radar.1 = bf16[2,8,2,8192]{3,2,1,0:T(2,128)(2,1)S(1)} custom-call(bf16[16,16384]{1,0:T(8,128)(2,1)} %bitcast.1, bf16[41,256,256]{2,1,0:T(8,128)(2,1)} %constant.2.clone.refs_1_), custom_call_target="tpu_custom_call" | custom-call | tf_op jit(solution)/shard_map/radar/pallas_call | solution.py:250
  29.0 0.8 %copy.4 = bf16[2,8,2,8192]{3,2,1,0:T(2,128)(2,1)} copy(bf16[2,8,2,8192]{3,2,1,0:T(2,128)(2,1)S(1)} %radar.1) | data formatting | bytes 1048576

commit v2 on v1

v2 whole, which is shorter than its diff:
```python
import math

import jax
import jax.numpy as jnp
import ml_dtypes
import numpy as np
from jax import lax
from jax.experimental import pallas as pl
from jax.experimental.pallas import tpu as pltpu
from jax.sharding import PartitionSpec as P

CHIRP = 1024
BANDS = 64
TAPS = 4096
MESH = pl.DeviceIdType.MESH

FRAME = 128
SPAN = 41
HALO = SPAN - 1
GROUP = 20
GROUPS = (SPAN - 1) // GROUP
APART = 16


def rounded(values):
    return np.asarray(values, np.float64).astype(ml_dtypes.bfloat16).astype(np.float64)


def weights():
    lag = np.arange(CHIRP)
    phase = math.pi * ((lag - CHIRP // 2) ** 2 % (2 * CHIRP)) / CHIRP
    scale = 1.0 / math.sqrt(CHIRP)
    chirp = rounded(np.cos(phase) * scale) + 1j * rounded(np.sin(phase) * scale)
    tap = np.arange(TAPS)
    window = 0.5 - 0.5 * np.cos(2.0 * np.pi * (tap + 0.5) / TAPS)
    prototype = rounded(np.sinc((tap - (TAPS - 1) / 2.0) / BANDS) * window / math.sqrt(BANDS))
    column = np.arange(BANDS)
    angle = 2.0 * np.pi * (column[:, None] * column[None, :] % BANDS) / BANDS
    table = rounded(np.cos(angle)) - 1j * rounded(np.sin(angle))
    modulated = prototype[None, :] * np.tile(table, (1, TAPS // BANDS))
    length = 2 * TAPS
    filters = np.fft.ifft(
        np.fft.fft(modulated, length, axis=1) * np.fft.fft(chirp[::-1], length)[None, :], axis=1
    )[:, : TAPS + CHIRP - 1]
    samples = SPAN * FRAME
    placed = np.zeros((2, samples, BANDS), np.complex128)
    for parity in range(2):
        first = (SPAN - 1) * FRAME + (parity + 1) * BANDS - (TAPS + CHIRP - 1)
        placed[parity, first : first + TAPS + CHIRP - 1] = filters.T
    real, imag = placed.real, placed.imag
    parts = np.stack(
        [np.stack([real, imag], axis=2), np.stack([-imag, real], axis=2)]
    )
    parts = parts.reshape(2, 2, SPAN, FRAME, 2, BANDS // 2, 2)
    parts = parts.transpose(2, 0, 3, 1, 6, 4, 5)
    return parts.reshape(SPAN, 2 * FRAME, 4 * BANDS).astype(np.float32).astype(ml_dtypes.bfloat16)


def kernel(
    count, x_ref, w_ref, o_ref, own, weight, tiles, total, times, turned, outgoing,
    own_sem, weight_sem, halo_send, halo_recv, send_sem, recv_sem, local_sem,
):
    me = lax.axis_index("tm")
    frames = own.shape[1] // FRAME - HALO
    half = frames // 2
    block = APART * 16

    load = pltpu.make_async_copy(
        x_ref, own.at[:, pl.ds(HALO * FRAME, frames * FRAME)], own_sem
    )
    load.start()

    def weight_load(group):
        piece = pl.ds(0, 1) if group is None else pl.ds(1 + group * GROUP, GROUP)
        sem = weight_sem.at[GROUPS if group is None else group]
        return pltpu.make_async_copy(w_ref.at[piece], weight.at[piece], sem)

    for group in reversed(range(GROUPS)):
        weight_load(group).start()
    weight_load(None).start()

    barrier = pltpu.get_barrier_semaphore()
    for shift in range(1, count):
        pl.semaphore_signal(
            barrier, inc=1, device_id={"tm": lax.rem(me + shift, count)}, device_id_type=MESH
        )

    def edge(group):
        first = 1 + group * GROUP if group else 0
        size = (HALO if group == GROUPS - 1 else 1 + (group + 1) * GROUP) - first
        return pltpu.make_async_remote_copy(
            src_ref=x_ref.at[:, pl.ds((frames - HALO + first) * FRAME, size * FRAME)],
            dst_ref=own.at[:, pl.ds(first * FRAME, size * FRAME)],
            send_sem=halo_send.at[group],
            recv_sem=halo_recv.at[group],
            device_id={"tm": lax.rem(me + 1, count)},
            device_id_type=MESH,
        )

    def greet():
        pl.semaphore_wait(barrier, count - 1)

        @pl.when(me < count - 1)
        def _():
            for group in reversed(range(GROUPS)):
                edge(group).start()

    def arrange(first, last):
        def one(index, carry):
            four = [
                own[:, pl.ds(pl.multiple_of((index + j * APART) * FRAME, FRAME), FRAME)].astype(
                    jnp.float32
                )
                for j in range(4)
            ]
            for rows in range(2):
                tiles[rows, index] = jnp.concatenate(
                    [
                        jnp.concatenate(
                            [f[part * 8 + rows * 4 : part * 8 + rows * 4 + 4] for f in four], axis=0
                        )
                        for part in range(2)
                    ],
                    axis=1,
                ).astype(jnp.bfloat16)
            return carry

        lax.fori_loop(first, last, one, 0, unroll=7)

    def product(side, rows, lag, amount):
        left = jnp.concatenate(
            [
                tiles[rows, pl.ds(side * half + lag + j, APART)].reshape(block, 2 * FRAME)
                for j in range(amount)
            ],
            axis=1,
        )
        right = weight[pl.ds(lag, amount)].reshape(amount * 2 * FRAME, 4 * BANDS)
        return jnp.dot(left, right, preferred_element_type=jnp.float32)

    def send(side, rows, chunk, shift):
        to = lax.rem(me + shift, count)
        start = pl.multiple_of((me * 2 + side) * frames, frames)
        return pltpu.make_async_remote_copy(
            src_ref=outgoing.at[chunk, :, to],
            dst_ref=o_ref.at[:, pl.ds(rows * 4, 4), :, pl.ds(start, frames)],
            send_sem=send_sem.at[chunk],
            recv_sem=recv_sem.at[chunk],
            device_id={"tm": to},
            device_id_type=MESH,
        )

    def keep(side, rows, chunk):
        start = pl.multiple_of((me * 2 + side) * frames, frames)
        return pltpu.make_async_copy(
            outgoing.at[chunk, :, me],
            o_ref.at[:, pl.ds(rows * 4, 4), :, pl.ds(start, frames)],
            local_sem.at[chunk],
        )

    load.wait()
    arrange(half, HALO + frames - 3 * APART)
    greet()

    def one_chunk(chunk, carry):
        side, rows = 1 - chunk // 2, chunk % 2
        total[...] = jnp.zeros_like(total)

        def one_group(step, carry):
            group = GROUPS - 1 - step

            @pl.when(chunk == 0)
            def _():
                weight_load(group).wait()

            for part in range(GROUPS):
                @pl.when((chunk == 2) & (group == part))
                def _():
                    @pl.when(me > 0)
                    def _():
                        edge(part).wait_recv()

                    if part == GROUPS - 1:
                        @pl.when(me == 0)
                        def _():
                            own[:, : HALO * FRAME] = jnp.zeros((16, HALO * FRAME), own.dtype)

                    arrange(
                        1 + part * GROUP if part else 0,
                        HALO + APART if part == GROUPS - 1 else 1 + (part + 1) * GROUP,
                    )

            total[...] += product(side, rows, 1 + group * GROUP, GROUP)
            return carry

        lax.fori_loop(0, GROUPS, one_group, 0)

        @pl.when(chunk == 0)
        def _():
            weight_load(None).wait()

        total[...] += product(side, rows, 0, 1)

        for v in range(APART):
            for upper in range(2):
                for parity in range(2):
                    row = (upper * 2 * APART + v * 2 + parity) * 8
                    times[row : row + 8, :] = total[
                        v * 16 + upper * 8 : v * 16 + upper * 8 + 8,
                        parity * 128 : parity * 128 + 128,
                    ]
        for r in range(4):
            across = jnp.concatenate(
                [
                    times[pl.ds(j // 2 * 16 * APART + j % 2 * 4 + r, 2 * APART, stride=8), :]
                    for j in range(4)
                ],
                axis=0,
            ).T
            for band in range(2):
                turned[pl.ds(2 * r + band, 2 * count, stride=8), :] = across[
                    band * 64 : band * 64 + 64
                ]
        outgoing[chunk] = turned[...].astype(jnp.bfloat16).reshape(2, count, 4, 2, frames)
        for shift in range(1, count):
            send(side, rows, chunk, shift).start()
        keep(side, rows, chunk).start()
        return carry

    lax.fori_loop(0, 4, one_chunk, 0)

    @pl.when(me < count - 1)
    def _():
        for group in range(GROUPS):
            edge(group).wait_send()

    def finish(chunk, carry):
        side, rows = 1 - chunk // 2, chunk % 2
        others = outgoing.at[chunk, :, pl.ds(0, count - 1)]
        pltpu.make_async_copy(others, others, recv_sem.at[chunk]).wait()
        pltpu.make_async_copy(others, others, send_sem.at[chunk]).wait()
        keep(side, rows, chunk).wait()
        return carry

    lax.fori_loop(0, 4, finish, 0)


def solution(mesh):
    count = mesh.shape["tm"]
    table = weights()

    def shards(echoes):
        parts, rows, samples = echoes.shape
        frames = samples // FRAME
        result = pl.pallas_call(
            lambda *refs: kernel(count, *refs),
            out_shape=pltpu.VMEM((2, rows, 2, count * 2 * frames), jnp.bfloat16),
            in_specs=[pl.BlockSpec(memory_space=pl.ANY)] * 2,
            out_specs=pl.BlockSpec(memory_space=pltpu.VMEM),
            scratch_shapes=[
                pltpu.VMEM((16, HALO * FRAME + samples), jnp.bfloat16),
                pltpu.VMEM(table.shape, jnp.bfloat16),
                pltpu.VMEM((2, HALO + frames - 3 * APART, 16, 2 * FRAME), jnp.bfloat16),
                pltpu.VMEM((APART * 16, 4 * BANDS), jnp.float32),
                pltpu.VMEM((frames * 4, 2 * BANDS), jnp.float32),
                pltpu.VMEM((2 * count * 8, frames), jnp.float32),
                pltpu.VMEM((4, 2, count, 4, 2, frames), jnp.bfloat16),
                pltpu.SemaphoreType.DMA,
                pltpu.SemaphoreType.DMA((GROUPS + 1,)),
                pltpu.SemaphoreType.DMA((GROUPS,)),
                pltpu.SemaphoreType.DMA((GROUPS,)),
                pltpu.SemaphoreType.DMA((4,)),
                pltpu.SemaphoreType.DMA((4,)),
                pltpu.SemaphoreType.DMA((4,)),
            ],
            compiler_params=pltpu.CompilerParams(
                collective_id=0, has_side_effects=True, vmem_limit_bytes=60 << 20
            ),
            name="radar",
        )(echoes.reshape(parts * rows, samples), jnp.asarray(table))
        return result

    return jax.shard_map(
        shards,
        mesh=mesh,
        in_specs=(P(None, "cp", "tm"),),
        out_specs=P(None, "cp", "tm", None),
        check_vma=False,
    )
```

time: 29.9 us -> 27.7 us (0.926)
  the two profiles are of different devices: /device:TPU:8 before, /device:TPU:2 now
where the time goes in v2:
time: 27.7 us; the launch traced here: 27.6 us
  Pallas kernels  26.8 us (97%)
  local copies, waits for them, and re-layouts  0.8 us (3%)
    pallas_call x1, Pallas kernels, shards(): pl.pallas_call(lambda *refs: kernel(count, *refs), out_shape=pltpu.VMEM((...  26.8 us
    unnamed x1, local copies, waits for them, and re-layouts  0.8 us

profile of v2, /device:TPU:2, one launch (start us, length us, event | category | flops | bytes accessed | tf_op | source)
XLA Modules:
  0.0 27.6 jit_solution(12567364788423243417)
XLA Ops:
  0.0 26.8 %radar.1 = bf16[2,8,2,8192]{3,2,1,0:T(2,128)(2,1)S(1)} custom-call(bf16[16,16384]{1,0:T(8,128)(2,1)} %bitcast.1, bf16[41,256,256]{2,1,0:T(8,128)(2,1)} %constant.2.clone.refs_1_), custom_call_target="tpu_custom_call" | custom-call | tf_op jit(solution)/shard_map/radar/pallas_call | solution.py:255
  26.8 0.8 %copy.4 = bf16[2,8,2,8192]{3,2,1,0:T(2,128)(2,1)} copy(bf16[2,8,2,8192]{3,2,1,0:T(2,128)(2,1)S(1)} %radar.1) | data formatting | bytes 1048576

commit v3 on v2

--- a/solution.py
+++ b/solution.py
@@ -222,7 +222,7 @@
                     band * 64 : band * 64 + 64
                 ]
         outgoing[chunk] = turned[...].astype(jnp.bfloat16).reshape(2, count, 4, 2, frames)
-        for shift in range(1, count):
+        for shift in sorted(range(1, count), key=lambda s: (s % 8 < 4, -min(s % 8, 8 - s % 8))):
             send(side, rows, chunk, shift).start()
         keep(side, rows, chunk).start()
         return carry

time: 27.7 us -> 27.3 us (0.986)
  the two profiles are of different devices: /device:TPU:2 before, /device:TPU:192 now
where the time goes in v3:
time: 27.3 us; the launch traced here: 27.2 us
  Pallas kernels  26.4 us (97%)
  local copies, waits for them, and re-layouts  0.8 us (3%)
    pallas_call x1, Pallas kernels, shards(): pl.pallas_call(lambda *refs: kernel(count, *refs), out_shape=pltpu.VMEM((...  26.4 us
    unnamed x1, local copies, waits for them, and re-layouts  0.8 us

profile of v3, /device:TPU:192, one launch (start us, length us, event | category | flops | bytes accessed | tf_op | source)
XLA Modules:
  0.0 27.2 jit_solution(3715055970520740090)
XLA Ops:
  0.0 26.4 %radar.1 = bf16[2,8,2,8192]{3,2,1,0:T(2,128)(2,1)S(1)} custom-call(bf16[16,16384]{1,0:T(8,128)(2,1)} %bitcast.1, bf16[41,256,256]{2,1,0:T(8,128)(2,1)} %constant.2.clone.refs_1_), custom_call_target="tpu_custom_call" | custom-call | tf_op jit(solution)/shard_map/radar/pallas_call | solution.py:255
  26.4 0.8 %copy.4 = bf16[2,8,2,8192]{3,2,1,0:T(2,128)(2,1)} copy(bf16[2,8,2,8192]{3,2,1,0:T(2,128)(2,1)S(1)} %radar.1) | data formatting | bytes 1048576

commit v4 on v3

--- a/solution.py
+++ b/solution.py
@@ -158,9 +158,9 @@
             local_sem.at[chunk],
         )
 
+    greet()
     load.wait()
     arrange(half, HALO + frames - 3 * APART)
-    greet()
 
     def one_chunk(chunk, carry):
         side, rows = 1 - chunk // 2, chunk % 2

time: 27.3 us -> 27.2 us (level)
  the two profiles are of different devices: /device:TPU:192 before, /device:TPU:2 now
where the time goes in v4:
time: 27.2 us; the launch traced here: 27.1 us
  Pallas kernels  26.3 us (97%)
  local copies, waits for them, and re-layouts  0.8 us (3%)
    pallas_call x1, Pallas kernels, shards(): pl.pallas_call(lambda *refs: kernel(count, *refs), out_shape=pltpu.VMEM((...  26.3 us
    unnamed x1, local copies, waits for them, and re-layouts  0.8 us

profile of v4, /device:TPU:2, one launch (start us, length us, event | category | flops | bytes accessed | tf_op | source)
XLA Modules:
  0.0 27.1 jit_solution(13033465698923761775)
XLA Ops:
  0.0 26.3 %radar.1 = bf16[2,8,2,8192]{3,2,1,0:T(2,128)(2,1)S(1)} custom-call(bf16[16,16384]{1,0:T(8,128)(2,1)} %bitcast.1, bf16[41,256,256]{2,1,0:T(8,128)(2,1)} %constant.2.clone.refs_1_), custom_call_target="tpu_custom_call" | custom-call | tf_op jit(solution)/shard_map/radar/pallas_call | solution.py:255
  26.3 0.8 %copy.4 = bf16[2,8,2,8192]{3,2,1,0:T(2,128)(2,1)} copy(bf16[2,8,2,8192]{3,2,1,0:T(2,128)(2,1)S(1)} %radar.1) | data formatting | bytes 1048576
